TPU v7x, 256 devices: a whole 4x4x8 slice. The times are simulated.
256 devices in a mesh: tm: 16 (over z_hi, x, core), head: 16 (over y, z_lo).
Axes of the slice: x: 4, y: 4, z: 8 (z_hi: 2, z_lo: 4; z = z_hi * 4 + z_lo), core: 2. Of those that a mesh axis runs over, the one named last changes fastest.
Arguments:
- queries: bfloat16 [65536, 4096], P(('tm', 'head')), may hold values from -512 to 512, as said below
- key_in: bfloat16 [65536, 4096], P(('tm', 'head')), may hold values from -512 to 512
- values_in: bfloat16 [65536, 4096], P(('tm', 'head')), may hold values from -6 to 6
- query_gain: float32 [4096], replicated, may hold values from 0.1 to 1.9
- key_gain: float32 [4096], replicated, may hold values from 0.1 to 1.9
- keep_list: int32 [1024, 32], P('tm'), may hold values from 0 to 1023, as said below
- counts: int32 [1024], P('tm'), may hold values from 1 to 32, as said below
Outputs:
- attended: bfloat16 [65536, 4096], P(('tm', 'head'))
Inputs may be any that keep to these rules, and one draw needn't show every extreme that they name: `queries`: the hidden rows of the two fields may coincide in places. `keep_list`: row t names 32 distinct blocks; the first is block t itself, the others lie in the frame of block t or in the frames just before and after it (block b lies in frame b // 32). Only the first counts[t] entries of row t of keep_list are used. The counts differ from frame to frame; some block uses all 32.
All inputs are finite; a program needn't handle non-finite values.
Results may differ from a plain program's by a relative error of at most 0.012.
Values may be sent and summed in bfloat16 or wider, within the bound.
A program may use at most 128 MiB of HBM per device.

v0:
```python
import jax
import jax.numpy as jnp
from jax import lax
from jax.sharding import PartitionSpec as P

HEADS = 32
HEAD_DIM = 128
BLOCK = 64
FRAME_BLOCKS = 32


def extended_2(block, sides, width):
    for axis, dim in sides:
        count = lax.axis_size(axis)
        forward = [(i, i + 1) for i in range(count - 1)]
        backward = [(target, source) for source, target in forward]
        low = lax.ppermute(
            lax.slice_in_dim(block, block.shape[dim] - width, None, axis=dim), axis, forward
        )
        high = lax.ppermute(lax.slice_in_dim(block, 0, width, axis=dim), axis, backward)
        block = jnp.concatenate([low, block, high], axis=dim)
    return block


def norm_rows(inputs, scaling):
    widened = inputs.astype(jnp.float32)
    mean_square = jnp.mean(widened * widened, axis=-1, keepdims=True)
    return (widened * lax.rsqrt(mean_square + 1e-06) * scaling).astype(jnp.bfloat16)


def shards(queries, key_in, values_in, query_gain, key_gain, keep_list, counts):
    frame_rows = FRAME_BLOCKS * BLOCK
    head_share = HEADS // lax.axis_size("head")
    query_normed = norm_rows(queries, query_gain)
    key_normed = norm_rows(key_in, key_gain)
    query_heads, key_heads, value_heads = (
        lax.all_to_all(query_normed, "head", split_axis=1, concat_axis=0, tiled=True),
        lax.all_to_all(key_normed, "head", split_axis=1, concat_axis=0, tiled=True),
        lax.all_to_all(values_in, "head", split_axis=1, concat_axis=0, tiled=True),
    )
    extended = extended_2(jnp.stack([key_heads, value_heads]), (("tm", 1),), frame_rows)
    local_rows = query_heads.shape[0]
    tile_count = local_rows // BLOCK
    frames_here = local_rows // frame_rows
    first_block = (lax.axis_index("tm") * frames_here - 1) * FRAME_BLOCKS
    local_ids = keep_list - first_block
    block_total = extended.shape[1] // BLOCK
    key_value_blocks = extended.reshape(2, block_total, BLOCK, head_share, HEAD_DIM)
    query_tiles = query_heads.reshape(tile_count, BLOCK, head_share, HEAD_DIM)
    scale_factor = HEAD_DIM ** (-0.5)

    def one_slot(slot_index, state_now):
        run_max, run_sum, totals = state_now
        block_ids = lax.dynamic_slice_in_dim(local_ids, slot_index, 1, 1)[:, 0]
        gathered = jnp.take(key_value_blocks, block_ids, axis=1)
        scores = (
            jnp.einsum(
                "tqhd,tkhd->thqk", query_tiles, gathered[0], preferred_element_type=jnp.float32
            )
            * scale_factor
        )
        scores = jnp.where((slot_index < counts)[:, None, None, None], scores, -1e30)
        new_max = jnp.maximum(run_max, jnp.max(scores, axis=-1))
        rescale = jnp.exp(run_max - new_max)
        weights = jnp.exp(scores - new_max[..., None]).astype(jnp.bfloat16)
        run_sum = run_sum * rescale + jnp.sum(weights.astype(jnp.float32), axis=-1)
        totals = totals * jnp.transpose(rescale, (0, 2, 1))[..., None] + jnp.einsum(
            "thqk,tkhd->tqhd", weights, gathered[1], preferred_element_type=jnp.float32
        )
        return (new_max, run_sum, totals)

    start_state = (
        jnp.full((tile_count, head_share, BLOCK), -1e30, jnp.float32),
        jnp.zeros((tile_count, head_share, BLOCK), jnp.float32),
        jnp.zeros((tile_count, BLOCK, head_share, HEAD_DIM), jnp.float32),
    )
    slot_limit = keep_list.shape[1]
    run_max, run_sum, totals = lax.fori_loop(0, slot_limit, one_slot, start_state)
    mixed_out = (totals / jnp.transpose(run_sum, (0, 2, 1))[..., None]).astype(jnp.bfloat16)
    mixed_out = mixed_out.reshape(local_rows, head_share * HEAD_DIM)
    return lax.all_to_all(mixed_out, "head", split_axis=0, concat_axis=1, tiled=True)


def solution(mesh):
    placed = (
        P(("tm", "head"), None),
        P(("tm", "head"), None),
        P(("tm", "head"), None),
        P(),
        P(),
        P("tm", None),
        P("tm"),
    )
    return jax.shard_map(
        shards, mesh=mesh, in_specs=placed, out_specs=P(("tm", "head"), None), check_vma=False
    )
```

profile of v0, /device:TPU:7, one launch (start us, length us, event | category | flops | bytes accessed | tf_op | source)
XLA Modules:
  0.0 858.5 jit_solution(5384086674345516937)
XLA Ops:
  5.6 8.4 all-to-all-start
  18.2 45.6 %all-to-all-done = bf16[256,16,256]{0,2,1:T(8,128)(2,1)} async-done(((bf16[256,16,256]{0,2,1:T(8,128)(2,1)}), bf16[256,16,256]{0,2,1:T(8,128)(2,1)}, u32[]{:S(2)}, u32[]{:S(2)}) %all-to-all-start) | async-done | bytes 2097184 | tf_op jit(solution)/shard_map/all_to_all | solution.py:38
  71.1 46.9 %all-to-all-done.1 = bf16[256,16,256]{0,2,1:T(8,128)(2,1)} async-done(((bf16[256,16,256]{0,2,1:T(8,128)(2,1)}), bf16[256,16,256]{0,2,1:T(8,128)(2,1)}, u32[]{:S(2)}, u32[]{:S(2)}) %all-to-all-start.1) | async-done | bytes 2097184 | tf_op jit(solution)/shard_map/all_to_all | solution.py:39
  134.0 7.4 collective-permute-start
  143.6 51.2 %all-to-all-done.2 = bf16[256,16,256]{2,0,1:T(8,128)(2,1)} async-done(((bf16[256,16,256]{2,0,1:T(8,128)(2,1)}), bf16[256,16,256]{2,0,1:T(8,128)(2,1)}, u32[]{:S(2)}, u32[]{:S(2)}) %all-to-all-start.2) | async-done | bytes 2097184 | tf_op jit(solution)/shard_map/all_to_all | solution.py:37
  201.5 18.3 %pad_maximum_fusion = bf16[2,8192,256]{2,1,0:T(8,128)(2,1)} fusion(bf16[2,2048,256]{2,1,0:T(8,128)(2,1)} %collective-permute-done.1, bf16[1,4096,256]{2,1,0:T(8,128)(2,1)S(1)} %bitcast.67, bf16[1,4096,256]{2,1,0:T(8,128)(2,1)S(1)} %bitcast.65, bf16[2,2048,256]{2,1,0:T(8,128)(2,1)} %collective-permute-done), kind=kLoop, calls=%fused_computation.24 | loop fusion | flops 33554432 | bytes 16777216 | tf_op jit(solution)/shard_map/concatenate | solution.py:21
  219.9 12.5 %reshape.55 = bf16[2,128,64,2,128]{4,3,2,1,0:T(2,128)(2,1)} reshape(bf16[2,8192,256]{2,1,0:T(8,128)(2,1)} %pad_maximum_fusion) | data formatting | bytes 16777216 | tf_op jit(solution)/shard_map/reshape | solution.py:48
  232.4 9.0 %copy.31 = bf16[2,128,64,2,128]{4,2,3,1,0:T(8,128)(2,1)} copy(bf16[2,128,64,2,128]{4,3,2,1,0:T(2,128)(2,1)} %reshape.55) | data formatting | bytes 16777216
  241.4 546.8 %while.18 = (s32[]{:T(128)}, f32[64,2,64]{2,1,0:T(2,128)S(1)}, f32[64,2,64]{2,1,0:T(2,128)S(1)}, f32[64,64,2,128]{3,1,2,0:T(8,128)}, s32[64]{0:T(128)S(1)}, /*in...) while((s32[]{:T(128)}, f32[64,2,64]{2,1,0:T(2,128)S(1)}, ...), condition=%wide.region_5.6_spmd.clone, body=%wide.region_2.5_spmd.clone.sunk | while | flops 280544704 | bytes 73996976 | solution.py:78
  241.4 6.4 gather_fusion
  292.7 6.4 gather_fusion
  309.8 6.4 gather_fusion
  326.9 6.4 gather_fusion
  343.9 6.4 gather_fusion
  361.0 6.4 gather_fusion
  378.1 6.4 gather_fusion
  395.2 6.4 gather_fusion
  412.3 6.4 gather_fusion
  463.5 6.4 gather_fusion
  480.6 6.4 gather_fusion
  514.8 6.4 gather_fusion
  531.9 6.4 gather_fusion
  549.0 6.4 gather_fusion
  566.1 6.4 gather_fusion
  583.2 6.4 gather_fusion
  600.2 6.4 gather_fusion
  634.4 6.4 gather_fusion
  651.5 6.4 gather_fusion
  702.8 6.4 gather_fusion
  719.8 6.4 gather_fusion
  754.0 6.4 gather_fusion
  795.9 56.2 %all_to_all.67 = bf16[16,256,256]{2,1,0:T(8,128)(2,1)S(1)} all-to-all(bf16[16,256,256]{2,1,0:T(8,128)(2,1)} %all_to_all.59), channel_id=1, replica_groups=mesh['tm'=16,'head'=16] {'head'}, dimensions={0} | all-to-all | bytes 4194304 | tf_op jit(solution)/shard_map/all_to_all | solution.py:81
  (502 shorter events, 459.4 us)
Async XLA Ops:
  0.0 3.9 copy-start.6
  5.6 58.3 %all-to-all-start = ((bf16[256,16,256]{0,2,1:T(8,128)(2,1)}), bf16[256,16,256]{0,2,1:T(8,128)(2,1)}, u32[]{:S(2)}, u32[]{:S(2)}) async-start(bf16[256,16,256]{0,2,1:T(8,128)(2,1)} %bitcast.68), calls=%async_computation | async-start | bytes 4194304 | tf_op jit(solution)/shard_map/all_to_all | solution.py:38
  14.0 54.3 %copy-start.5 = (bf16[256,4096]{1,0:T(8,128)(2,1)S(1)}, bf16[256,4096]{1,0:T(8,128)(2,1)}, u32[]{:S(2)}) copy-start(bf16[256,4096]{1,0:T(8,128)(2,1)} %param.9) | copy-start | bytes 6291460
  18.2 50.6 %copy-start.7 = (f32[4096]{0:T(1024)S(1)}, f32[4096]{0:T(1024)}, u32[]{:S(2)}) copy-start(f32[4096]{0:T(1024)} %param.12) | copy-start | bytes 49156
  63.8 54.2 %all-to-all-start.1 = ((bf16[256,16,256]{0,2,1:T(8,128)(2,1)}), bf16[256,16,256]{0,2,1:T(8,128)(2,1)}, u32[]{:S(2)}, u32[]{:S(2)}) async-start(bf16[256,16,256]{0,2,1:T(8,128)(2,1)} %bitcast.70), calls=%async_computation.1 | async-start | bytes 4194304 | tf_op jit(solution)/shard_map/all_to_all | solution.py:39
  118.0 76.7 %all-to-all-start.2 = ((bf16[256,16,256]{2,0,1:T(8,128)(2,1)}), bf16[256,16,256]{2,0,1:T(8,128)(2,1)}, u32[]{:S(2)}, u32[]{:S(2)}) async-start(bf16[256,16,256]{2,0,1:T(8,128)(2,1)} %bitcast.41), calls=%async_computation.2 | async-start | bytes 4194304 | tf_op jit(solution)/shard_map/all_to_all | solution.py:37
  125.3 8.7 %copy-start.2 = (bf16[16,256,256]{2,1,0:T(8,128)(2,1)}, bf16[16,256,256]{2,1,0:T(8,128)(2,1)S(1)}, u32[]{:S(2)}) copy-start(bf16[16,256,256]{2,1,0:T(8,128)(2,1)S(1)} %copy.27) | copy-start | bytes 6291460
  129.8 13.7 %copy-start.8 = (s32[64,32]{0,1:T(8,128)S(1)}, s32[64,32]{0,1:T(8,128)}, u32[]{:S(2)}) copy-start(s32[64,32]{0,1:T(8,128)} %param.14) | copy-start | bytes 24580
  134.0 67.0 %collective-permute-start = (bf16[2,2048,256]{2,1,0:T(8,128)(2,1)}, bf16[2,2048,256]{2,1,0:T(8,128)(2,1)}, u32[]{:S(2)}, u32[]{:S(2)}) collective-permute-start(bf16[2,2048,256]{2,1,0:T(8,128)(2,1)} %get-tuple-element.220), channel_id=1, source_target_pairs={{0,16},{16,32},{32,48},{48,64},{64,80},{80,96},{96,112},{112,128},... | collective-permute-start | bytes 6291464 | tf_op jit(solution)/shard_map/ppermute | solution.py:17
  141.4 59.6 %collective-permute-start.1 = (bf16[2,2048,256]{2,1,0:T(8,128)(2,1)}, bf16[2,2048,256]{2,1,0:T(8,128)(2,1)}, u32[]{:S(2)}, u32[]{:S(2)}) collective-permute-start(bf16[2,2048,256]{2,1,0:T(8,128)(2,1)} %get-tuple-element.221), channel_id=1, source_target_pairs={{16,0},{32,16},{48,32},{64,48},{80,64},{96,80},{112,96},{128,112},... | collective-permute-start | bytes 6291464 | tf_op jit(solution)/shard_map/ppermute | solution.py:20
  198.7 2.3 copy-start.3
  198.7 2.9 copy-start.4
  232.4 9.0 %copy-start.9 = (s32[64]{0:T(128)S(1)}, s32[64]{0:T(128)}, u32[]{:S(2)}) copy-start(s32[64]{0:T(128)} %param.15) | copy-start | bytes 772
  250.5 2.2 copy-start
  267.6 2.2 copy-start
  284.7 2.2 copy-start
  301.7 2.2 copy-start
  318.8 2.2 copy-start
  335.9 2.2 copy-start
  353.0 2.2 copy-start
  370.1 2.2 copy-start
  387.2 2.2 copy-start
  404.3 2.2 copy-start
  421.3 2.2 copy-start
  438.4 2.2 copy-start
  455.5 2.2 copy-start
  506.8 2.2 copy-start
  609.3 2.2 copy-start
  626.4 2.2 copy-start
  677.6 2.2 copy-start
  694.7 2.2 copy-start
  746.0 2.2 copy-start
  (45 other events, 90.9 us)
where the time goes:
time: 863 us; the launch traced here: 858 us
  local copies, waits for them, and re-layouts  292 us (34%)
  other arithmetic  172 us (20%)
  matrix products  166 us (19%)
  waiting for transfers between devices  144 us (17%)
  blocking collectives  56.2 us (7%)
  starting transfers between devices  26.8 us (3%)
    gather x32, local copies, waits for them, and re-layouts, one_slot(): gathered = jnp.take(key_value_blocks, block_ids, axis=1)  206 us
    dot_general x32, matrix products, one_slot(): jnp.einsum('thqk,tkhd->tqhd', weights, gathered[1], preferred_element_typ...  123 us
    select_n x32, other arithmetic, one_slot(): gathered = jnp.take(key_value_blocks, block_ids, axis=1)  83.9 us
    all_to_all x1, blocking collectives, shards(): lax.all_to_all(mixed_out, 'head', split_axis=0, concat_axis=1, tiled=True)  56.2 us
    reduce_sum x32, other arithmetic, one_slot(): run_sum = run_sum * rescale + jnp.sum(weights.astype(jnp.float32), axis=-1)  52.4 us
    all_to_all x1, waiting for transfers between devices, shards(): lax.all_to_all(query_normed, 'head', split_axis=1, concat_axis=0, tiled=T...  51.2 us
    all_to_all x1, waiting for transfers between devices, shards(): lax.all_to_all(values_in, 'head', split_axis=1, concat_axis=0, tiled=True)  46.9 us
    all_to_all x1, waiting for transfers between devices, shards(): lax.all_to_all(key_normed, 'head', split_axis=1, concat_axis=0, tiled=True)  45.6 us
  transfers between devices with their start and end apart: 5, of which 3 were waited for; matrix products, arithmetic and copies ran while one was open for 3% of the time, Pallas kernels for 0%

commit v1 on v0

v1 whole, which is shorter than its diff:
```python
import functools
import math

import jax
import jax.numpy as jnp
from jax import lax
from jax.experimental import pallas as pl
from jax.experimental.pallas import tpu as pltpu
from jax.sharding import PartitionSpec as P

HEADS = 32
HEAD_DIM = 128
BLOCK = 64
FRAME_BLOCKS = 32
KEEP = 32
GROUP = 4
EXP2_SCALE = HEAD_DIM ** (-0.5) * math.log2(math.e)
NT = (((1,), (1,)), ((), ()))


def norm_rows(inputs, scaling):
    widened = inputs.astype(jnp.float32)
    mean_square = jnp.mean(widened * widened, axis=-1, keepdims=True)
    return (widened * lax.rsqrt(mean_square + 1e-06) * scaling).astype(jnp.bfloat16)


def attend_tile(q_ref, k_ref, v_ref, ones_ref, o_ref, ids_ref, count, first_block, t, groups):
    null_block = v_ref.shape[0] // BLOCK - 1
    own = ids_ref[t, 0] - first_block
    key_rows, value_rows, ones_rows = [], [], []
    for slot in range(groups * GROUP):
        live = slot < count
        block = ids_ref[t, slot] - first_block
        key_rows.append(pl.ds(pl.multiple_of(jnp.where(live, block, own) * BLOCK, BLOCK), BLOCK))
        value_rows.append(
            pl.ds(pl.multiple_of(jnp.where(live, block, null_block) * BLOCK, BLOCK), BLOCK)
        )
        ones_rows.append(pl.ds(pl.multiple_of(jnp.where(live, 0, BLOCK), BLOCK), BLOCK))
    rows = pl.ds(pl.multiple_of(t * BLOCK, BLOCK), BLOCK)
    heads = [slice(h * HEAD_DIM, (h + 1) * HEAD_DIM) for h in range(2)]
    scores = []
    for lanes in heads:
        query = q_ref[rows, lanes]
        of_head = []
        for g in range(groups):
            slots = range(g * GROUP, (g + 1) * GROUP)
            keys = jnp.concatenate([k_ref[key_rows[s], lanes] for s in slots], axis=0)
            of_head.append(
                lax.dot_general(query, keys, NT, preferred_element_type=jnp.float32)
            )
        scores.append(of_head)
    for lanes, of_head in zip(heads, scores):
        peak = jnp.max(functools.reduce(jnp.maximum, of_head), axis=1, keepdims=True)
        total = jnp.zeros((BLOCK, 2 * HEAD_DIM), jnp.float32)
        for g in range(groups):
            weights = jnp.exp2((of_head[g] - peak) * EXP2_SCALE).astype(jnp.bfloat16)
            slots = range(g * GROUP, (g + 1) * GROUP)
            values = jnp.concatenate(
                [
                    jnp.concatenate([v_ref[value_rows[s], lanes], ones_ref[ones_rows[s], :]], axis=1)
                    for s in slots
                ],
                axis=0,
            )
            total = total + jnp.dot(weights, values, preferred_element_type=jnp.float32)
        o_ref[rows, lanes] = (total[:, :HEAD_DIM] / total[:, HEAD_DIM:]).astype(jnp.bfloat16)


def attend_kernel(
    ids_ref, counts_ref, first_ref, q_in, k_low, k_own, k_high, v_low, v_own, v_high,
    o_ref, q_ref, k_ref, v_ref, ones_ref, sems,
):
    frame_rows = FRAME_BLOCKS * BLOCK
    local_rows = q_in.shape[0]
    copies = []
    plan = [(q_in, q_ref.at[pl.ds(0, local_rows)])]
    for low, own, high, dest in ((k_low, k_own, k_high, k_ref), (v_low, v_own, v_high, v_ref)):
        plan.append((low, dest.at[pl.ds(0, frame_rows)]))
        plan.append((own, dest.at[pl.ds(frame_rows, local_rows)]))
        plan.append((high, dest.at[pl.ds(frame_rows + local_rows, frame_rows)]))
    for index, (source, dest) in enumerate(plan):
        copy = pltpu.make_async_copy(source, dest, sems.at[index])
        copy.start()
        copies.append(copy)
    null_row = local_rows + 2 * frame_rows
    v_ref[pl.ds(null_row, BLOCK), :] = jnp.zeros((BLOCK, v_ref.shape[1]), jnp.bfloat16)
    ones_ref[pl.ds(0, BLOCK), :] = jnp.ones((BLOCK, HEAD_DIM), jnp.bfloat16)
    ones_ref[pl.ds(BLOCK, BLOCK), :] = jnp.zeros((BLOCK, HEAD_DIM), jnp.bfloat16)
    for copy in copies:
        copy.wait()
    first_block = first_ref[0]

    def tile(t, carry):
        count = counts_ref[t]
        needed = (count + GROUP - 1) // GROUP
        for groups in range(1, KEEP // GROUP + 1):

            @pl.when(needed == groups)
            def _():
                attend_tile(
                    q_ref, k_ref, v_ref, ones_ref, o_ref, ids_ref, count, first_block, t, groups
                )

        return carry

    lax.fori_loop(0, local_rows // BLOCK, tile, 0)


def attend(keep_list, counts, first_block, query, key_parts, value_parts):
    frame_rows = FRAME_BLOCKS * BLOCK
    rows, width = query.shape
    scalar = pl.BlockSpec(memory_space=pltpu.SMEM)
    whole = pl.BlockSpec(memory_space=pl.ANY)
    reach = rows + 2 * frame_rows
    return pl.pallas_call(
        attend_kernel,
        out_shape=jax.ShapeDtypeStruct((rows, width), jnp.bfloat16),
        in_specs=[scalar] * 3 + [whole] * 7,
        out_specs=pl.BlockSpec(memory_space=pltpu.VMEM),
        scratch_shapes=[
            pltpu.VMEM((rows, width), jnp.bfloat16),
            pltpu.VMEM((reach, width), jnp.bfloat16),
            pltpu.VMEM((reach + BLOCK, width), jnp.bfloat16),
            pltpu.VMEM((2 * BLOCK, HEAD_DIM), jnp.bfloat16),
            pltpu.SemaphoreType.DMA((7,)),
        ],
        compiler_params=pltpu.CompilerParams(vmem_limit_bytes=48 * 2**20),
        cost_estimate=pl.CostEstimate(
            flops=rows * KEEP * BLOCK * width * 4,
            bytes_accessed=2 * (2 * rows + 2 * reach) * width,
            transcendentals=rows * KEEP * BLOCK * 2,
        ),
    )(keep_list, counts, first_block, query, *key_parts, *value_parts)


def with_neighbours(block):
    frame_rows = FRAME_BLOCKS * BLOCK
    count = lax.axis_size("tm")
    forward = [(i, i + 1) for i in range(count - 1)]
    backward = [(target, source) for source, target in forward]
    low = lax.ppermute(block[-frame_rows:], "tm", forward)
    high = lax.ppermute(block[:frame_rows], "tm", backward)
    return low, block, high


def to_heads(block):
    return lax.all_to_all(block, "head", split_axis=1, concat_axis=0, tiled=True)


def shards(queries, key_in, values_in, query_gain, key_gain, keep_list, counts):
    value_parts = with_neighbours(to_heads(values_in))
    key_parts = with_neighbours(to_heads(norm_rows(key_in, key_gain)))
    query = to_heads(norm_rows(queries, query_gain))
    frames_here = query.shape[0] // (FRAME_BLOCKS * BLOCK)
    first_block = (lax.axis_index("tm") * frames_here - 1) * FRAME_BLOCKS
    first_block = first_block.astype(jnp.int32).reshape(1)
    mixed_out = attend(keep_list, counts, first_block, query, key_parts, value_parts)
    return lax.all_to_all(mixed_out, "head", split_axis=0, concat_axis=1, tiled=True)


def solution(mesh):
    placed = (
        P(("tm", "head"), None),
        P(("tm", "head"), None),
        P(("tm", "head"), None),
        P(),
        P(),
        P("tm", None),
        P("tm"),
    )
    return jax.shard_map(
        shards, mesh=mesh, in_specs=placed, out_specs=P(("tm", "head"), None), check_vma=False
    )
```

time: 863 us -> 299 us (0.35)
  local copies, waits for them, and re-layouts: 292 us -> 14.1 us
  other arithmetic: 172 us -> 4.84 us
  matrix products: 166 us -> 0 us
  Pallas kernels: 0 us -> 53.6 us
  starting transfers between devices: 26.8 us -> 38.2 us
  blocking collectives: 56.2 us -> 46.3 us
    gather x32 -> x0, local copies, waits for them, and re-layouts: 206 us -> none  [one_slot(): gathered = jnp.take(key_value_blocks, block_ids, axis=1)]
    dot_general x64 -> x0, matrix products: 166 us -> none  [the longest x32 123 us: one_slot(): jnp.einsum('thqk,tkhd->tqhd', weights, gathered[1], preferred_element_typ...]
    select_n x32 -> x0, other arithmetic: 83.9 us -> none  [one_slot(): gathered = jnp.take(key_value_blocks, block_ids, axis=1)]
    pallas_call x0 -> x1, Pallas kernels: none -> 53.6 us  [attend(): pl.pallas_call(attend_kernel, out_shape=jax.ShapeDtypeStruct((rows, width...]
    reduce_sum x32 -> x0, other arithmetic: 52.4 us -> none  [one_slot(): run_sum = run_sum * rescale + jnp.sum(weights.astype(jnp.float32), axis=-1)]
    while x160 -> x0, local copies, waits for them, and re-layouts: 30.4 us -> none
    concatenate x1 -> x0, other arithmetic: 18.3 us -> none  [extended_2(): block = jnp.concatenate([low, block, high], axis=dim)]
    unnamed x20 -> x15, local copies, waits for them, and re-layouts: 19.4 us -> 1.62 us
  transfers between devices with their start and end apart: 5 -> 7, of which waited for: 3 -> 3; matrix products, arithmetic and copies ran while one was open for 3% -> 4% of each run, Pallas kernels for 0% -> 0%
where the time goes in v1:
time: 299 us; the launch traced here: 297 us
  waiting for transfers between devices  140 us (47%)
  Pallas kernels  53.6 us (18%)
  blocking collectives  46.3 us (15%)
  starting transfers between devices  38.2 us (13%)
  local copies, waits for them, and re-layouts  14.1 us (5%)
  other arithmetic  4.84 us (2%)
    all_to_all x3, waiting for transfers between devices, to_heads(): lax.all_to_all(block, 'head', split_axis=1, concat_axis=0, tiled=True)  140 us
    pallas_call x1, Pallas kernels, attend(): pl.pallas_call(attend_kernel, out_shape=jax.ShapeDtypeStruct((rows, width...  53.6 us
    all_to_all x1, blocking collectives, shards(): lax.all_to_all(mixed_out, 'head', split_axis=0, concat_axis=1, tiled=True)  46.3 us
    all_to_all x3, starting transfers between devices, to_heads(): lax.all_to_all(block, 'head', split_axis=1, concat_axis=0, tiled=True)  17.4 us
    ppermute x2, starting transfers between devices, with_neighbours(): low = lax.ppermute(block[-frame_rows:], 'tm', forward)  17 us
    all_to_all x3, local copies, waits for them, and re-layouts, to_heads(): lax.all_to_all(block, 'head', split_axis=1, concat_axis=0, tiled=True)  6.2 us
  transfers between devices with their start and end apart: 7, of which 3 were waited for; matrix products, arithmetic and copies ran while one was open for 4% of the time, Pallas kernels for 0%

profile of v1, /device:TPU:7, one launch (start us, length us, event | category | flops | bytes accessed | tf_op | source)
XLA Modules:
  0.0 297.1 jit_solution(12388314396955326358)
XLA Ops:
  0.0 2.2 fusion.3
  2.3 1.4 fusion.5
  3.6 1.5 copy.21
  5.1 8.4 %all-to-all-start.1 = ((bf16[256,16,256]{2,0,1:T(8,128)(2,1)}), bf16[256,16,256]{2,0,1:T(8,128)(2,1)S(1)}, u32[]{:S(2)}, u32[]{:S(2)}) async-start(bf16[256,16,256]{2,0,1:T(8,128)(2,1)} %bitcast.35), calls=%async_computation.1 | async-start | bytes 4194304 | tf_op jit(solution)/shard_map/all_to_all | solution.py:147
  13.5 3.1 %copy.20 = bf16[32,16,8,256]{3,2,0,1:T(8,128)(2,1)} copy(bf16[32,16,8,256]{3,2,1,0:T(8,128)(2,1)} %bitcast.37) | data formatting | bytes 4194304 | tf_op jit(solution)/shard_map/all_to_all | solution.py:147
  16.6 46.6 %all-to-all-done.1 = bf16[256,16,256]{2,0,1:T(8,128)(2,1)S(1)} async-done(((bf16[256,16,256]{2,0,1:T(8,128)(2,1)}), bf16[256,16,256]{2,0,1:T(8,128)(2,1)S(1)}, u32[]{:S(2)}, u32[]{:S(2)}) %all-to-all-start.1) | async-done | bytes 2097184 | tf_op jit(solution)/shard_map/all_to_all | solution.py:147
  63.3 1.3 copy-done.3
  64.6 4.6 %all-to-all-start.2 = ((bf16[256,16,256]{2,0,1:T(8,128)(2,1)}), bf16[256,16,256]{2,0,1:T(8,128)(2,1)}, u32[]{:S(2)}, u32[]{:S(2)}) async-start(bf16[256,16,256]{2,0,1:T(8,128)(2,1)} %bitcast.34), calls=%async_computation.2 | async-start | bytes 4194304 | tf_op jit(solution)/shard_map/all_to_all | solution.py:147
  69.2 0.0 copy-start.5
  69.2 0.5 fusion
  69.7 0.2 copy-done.5
  69.9 0.7 fusion.2
  70.7 1.5 copy.22
  72.2 46.7 %all-to-all-done.2 = bf16[256,16,256]{2,0,1:T(8,128)(2,1)} async-done(((bf16[256,16,256]{2,0,1:T(8,128)(2,1)}), bf16[256,16,256]{2,0,1:T(8,128)(2,1)}, u32[]{:S(2)}, u32[]{:S(2)}) %all-to-all-start.2) | async-done | bytes 2097184 | tf_op jit(solution)/shard_map/all_to_all | solution.py:147
  118.9 4.4 %all-to-all-start = ((bf16[256,16,256]{2,0,1:T(8,128)(2,1)}), bf16[256,16,256]{2,0,1:T(8,128)(2,1)}, u32[]{:S(2)}, u32[]{:S(2)}) async-start(bf16[256,16,256]{2,0,1:T(8,128)(2,1)} %bitcast.29), calls=%async_computation | async-start | bytes 4194304 | tf_op jit(solution)/shard_map/all_to_all | solution.py:147
  123.4 3.2 %fusion.6 = (bf16[8,256,256]{2,1,0:T(8,128)(2,1)}, bf16[8,256,256]{2,1,0:T(8,128)(2,1)}) fusion(bf16[16,256,256]{2,1,0:T(8,128)(2,1)} %bitcast.7), kind=kLoop, calls=%fused_computation.15 | loop fusion | bytes 4194304 | tf_op jit(solution)/shard_map/slice | solution.py:142
  126.6 7.4 %collective-permute-start.2 = (bf16[2048,256]{1,0:T(8,128)(2,1)}, bf16[2048,256]{1,0:T(8,128)(2,1)S(1)}, u32[]{:S(2)}, u32[]{:S(2)}) collective-permute-start(bf16[2048,256]{1,0:T(8,128)(2,1)} %bitcast.8), channel_id=1, source_target_pairs={{0,16},{16,32},{32,48},{48,64},{64,80},{80,96},{96,112},{112,128},... | collective-permute-start | bytes 3145736 | tf_op jit(solution)/shard_map/ppermute | solution.py:141
  134.0 1.9 collective-permute-start.3
  135.9 0.0 copy-start.6
  135.9 0.0 copy-start
  135.9 1.6 fusion.7
  137.5 9.6 %collective-permute-start = (bf16[2048,256]{1,0:T(8,128)(2,1)}, bf16[2048,256]{1,0:T(8,128)(2,1)S(1)}, u32[]{:S(2)}, u32[]{:S(2)}) collective-permute-start(bf16[2048,256]{1,0:T(8,128)(2,1)} %bitcast.4), channel_id=1, source_target_pairs={{0,16},{16,32},{32,48},{48,64},{64,80},{80,96},{96,112},{112,128},... | collective-permute-start | bytes 3145736 | tf_op jit(solution)/shard_map/ppermute | solution.py:141
  147.1 1.9 collective-permute-start.1
  149.1 0.1 copy.11.ids_ref
  149.1 46.5 %all-to-all-done = bf16[256,16,256]{2,0,1:T(8,128)(2,1)} async-done(((bf16[256,16,256]{2,0,1:T(8,128)(2,1)}), bf16[256,16,256]{2,0,1:T(8,128)(2,1)}, u32[]{:S(2)}, u32[]{:S(2)}) %all-to-all-start) | async-done | bytes 2097184 | tf_op jit(solution)/shard_map/all_to_all | solution.py:147
  195.6 0.0 collective-permute-done.2.v_low
  195.6 0.0 collective-permute-done.3.v_high
  195.6 0.0 collective-permute-done.k_low
  195.7 0.0 collective-permute-done.1.k_high
  195.7 53.6 %shard_map.73 = bf16[4096,256]{1,0:T(8,128)(2,1)} custom-call(s32[64,32]{1,0:T(8,128)S(1)} %copy.11.ids_ref, s32[64]{0:T(128)S(1)} %copy-done, s32[1]{0:T(128)} %bitcast.first_ref, bf16[4096,256]{1,0:T(8,128)(2,1)} %bitcast.2.q_in, bf16[2048,256]{1,0:T(8,128)(2,1)S(1)} %collective-permute-done.k_low, bf16[4096,256]{1,0:T(8,128)(2,1)} %bitcast.32, ...), custom_call_target="tpu_custom_call" | custom-call | flops 8589934592 | bytes 12582912 | tf_op jit(solution)/shard_map/pallas_call | solution.py:115
  249.3 46.3 %all_to_all.76 = bf16[16,256,256]{2,1,0:T(8,128)(2,1)S(1)} all-to-all(bf16[16,256,256]{2,1,0:T(8,128)(2,1)} %bitcast.38), channel_id=1, replica_groups=mesh['tm'=16,'head'=16] {'head'}, dimensions={0} | all-to-all | bytes 4194304 | tf_op jit(solution)/shard_map/all_to_all | solution.py:158
  295.6 1.6 copy.16
  (11 shorter events, 0.0 us)
Async XLA Ops:
  0.0 2.2 copy-start.1
  5.1 58.2 %all-to-all-start.1 = ((bf16[256,16,256]{2,0,1:T(8,128)(2,1)}), bf16[256,16,256]{2,0,1:T(8,128)(2,1)S(1)}, u32[]{:S(2)}, u32[]{:S(2)}) async-start(bf16[256,16,256]{2,0,1:T(8,128)(2,1)} %bitcast.35), calls=%async_computation.1 | async-start | bytes 4194304 | tf_op jit(solution)/shard_map/all_to_all | solution.py:147
  63.3 1.3 copy-start.3
  64.6 4.6 %copy-start.2 = (bf16[256,4096]{1,0:T(8,128)(2,1)S(1)}, bf16[256,4096]{1,0:T(8,128)(2,1)}, u32[]{:S(2)}) copy-start(bf16[256,4096]{1,0:T(8,128)(2,1)} %param.7) | copy-start | bytes 6291460
  64.6 54.3 %all-to-all-start.2 = ((bf16[256,16,256]{2,0,1:T(8,128)(2,1)}), bf16[256,16,256]{2,0,1:T(8,128)(2,1)}, u32[]{:S(2)}, u32[]{:S(2)}) async-start(bf16[256,16,256]{2,0,1:T(8,128)(2,1)} %bitcast.34), calls=%async_computation.2 | async-start | bytes 4194304 | tf_op jit(solution)/shard_map/all_to_all | solution.py:147
  69.2 0.7 copy-start.5
  118.9 76.7 %all-to-all-start = ((bf16[256,16,256]{2,0,1:T(8,128)(2,1)}), bf16[256,16,256]{2,0,1:T(8,128)(2,1)}, u32[]{:S(2)}, u32[]{:S(2)}) async-start(bf16[256,16,256]{2,0,1:T(8,128)(2,1)} %bitcast.29), calls=%async_computation | async-start | bytes 4194304 | tf_op jit(solution)/shard_map/all_to_all | solution.py:147
  123.4 12.5 %copy-start.4 = (bf16[256,16,256]{2,0,1:T(8,128)(2,1)S(1)}, bf16[256,16,256]{2,0,1:T(8,128)(2,1)}, u32[]{:S(2)}) copy-start(bf16[256,16,256]{2,0,1:T(8,128)(2,1)} %copy-done.3) | copy-start | bytes 6291460
  126.6 69.1 %collective-permute-start.2 = (bf16[2048,256]{1,0:T(8,128)(2,1)}, bf16[2048,256]{1,0:T(8,128)(2,1)S(1)}, u32[]{:S(2)}, u32[]{:S(2)}) collective-permute-start(bf16[2048,256]{1,0:T(8,128)(2,1)} %bitcast.8), channel_id=1, source_target_pairs={{0,16},{16,32},{32,48},{48,64},{64,80},{80,96},{96,112},{112,128},... | collective-permute-start | bytes 3145736 | tf_op jit(solution)/shard_map/ppermute | solution.py:141
  134.0 61.7 %collective-permute-start.3 = (bf16[2048,256]{1,0:T(8,128)(2,1)}, bf16[2048,256]{1,0:T(8,128)(2,1)S(1)}, u32[]{:S(2)}, u32[]{:S(2)}) collective-permute-start(bf16[2048,256]{1,0:T(8,128)(2,1)} %bitcast.10), channel_id=1, source_target_pairs={{16,0},{32,16},{48,32},{64,48},{80,64},{96,80},{112,96},{128,112},... | collective-permute-start | bytes 3145736 | tf_op jit(solution)/shard_map/ppermute | solution.py:142
  135.9 13.2 %copy-start.6 = (s32[64,32]{0,1:T(8,128)S(1)}, s32[64,32]{0,1:T(8,128)}, u32[]{:S(2)}) copy-start(s32[64,32]{0,1:T(8,128)} %param.12) | copy-start | bytes 24580
  135.9 59.8 %copy-start = (s32[64]{0:T(128)S(1)}, s32[64]{0:T(128)}, u32[]{:S(2)}) copy-start(s32[64]{0:T(128)} %counts_ref.1) | copy-start | bytes 772
  137.5 58.2 %collective-permute-start = (bf16[2048,256]{1,0:T(8,128)(2,1)}, bf16[2048,256]{1,0:T(8,128)(2,1)S(1)}, u32[]{:S(2)}, u32[]{:S(2)}) collective-permute-start(bf16[2048,256]{1,0:T(8,128)(2,1)} %bitcast.4), channel_id=1, source_target_pairs={{0,16},{16,32},{32,48},{48,64},{64,80},{80,96},{96,112},{112,128},... | collective-permute-start | bytes 3145736 | tf_op jit(solution)/shard_map/ppermute | solution.py:141
  147.1 48.5 %collective-permute-start.1 = (bf16[2048,256]{1,0:T(8,128)(2,1)}, bf16[2048,256]{1,0:T(8,128)(2,1)}, u32[]{:S(2)}, u32[]{:S(2)}) collective-permute-start(bf16[2048,256]{1,0:T(8,128)(2,1)} %bitcast.6), channel_id=1, source_target_pairs={{16,0},{32,16},{48,32},{64,48},{80,64},{96,80},{112,96},{128,112},... | collective-permute-start | bytes 3145736 | tf_op jit(solution)/shard_map/ppermute | solution.py:142

commit v2 on v0

v2 whole, which is shorter than its diff:
```python
import functools
import math

import jax
import jax.numpy as jnp
from jax import lax
from jax.experimental import pallas as pl
from jax.experimental.pallas import tpu as pltpu
from jax.sharding import PartitionSpec as P

HEADS = 32
HEAD_DIM = 128
BLOCK = 64
FRAME_BLOCKS = 32
KEEP = 32
LINE = 4
GROUP = 4
EXP2_SCALE = HEAD_DIM ** (-0.5) * math.log2(math.e)
NT = (((1,), (1,)), ((), ()))


def attend_tile(q_ref, k_ref, v_ref, ones_ref, o_ref, slots_ref, t, groups):
    heads = [slice(h * HEAD_DIM, (h + 1) * HEAD_DIM) for h in range(2)]
    scores = []
    for lanes in heads:
        query = q_ref[t, :, lanes]
        of_head = []
        for g in range(groups):
            slots = range(g * GROUP, (g + 1) * GROUP)
            keys = jnp.concatenate([k_ref[slots_ref[t, s], :, lanes] for s in slots], axis=0)
            of_head.append(
                lax.dot_general(query, keys, NT, preferred_element_type=jnp.float32)
            )
        scores.append(of_head)
    for lanes, of_head in zip(heads, scores):
        peak = jnp.max(functools.reduce(jnp.maximum, of_head), axis=1, keepdims=True)
        total = jnp.zeros((BLOCK, 2 * HEAD_DIM), jnp.float32)
        for g in range(groups):
            weights = jnp.exp2((of_head[g] - peak) * EXP2_SCALE).astype(jnp.bfloat16)
            slots = range(g * GROUP, (g + 1) * GROUP)
            values = jnp.concatenate(
                [
                    jnp.concatenate(
                        [
                            v_ref[slots_ref[t, KEEP + s], :, lanes],
                            ones_ref[slots_ref[t, 2 * KEEP + s]],
                        ],
                        axis=1,
                    )
                    for s in slots
                ],
                axis=0,
            )
            total = total + jnp.dot(weights, values, preferred_element_type=jnp.float32)
        o_ref[t, :, lanes] = (total[:, :HEAD_DIM] / total[:, HEAD_DIM:]).astype(jnp.bfloat16)


def slot_table(keep_list, counts, first_block, null_block):
    live = jnp.arange(KEEP, dtype=jnp.int32)[None, :] < counts[:, None]
    local = keep_list - first_block
    own = FRAME_BLOCKS + jnp.arange(keep_list.shape[0], dtype=jnp.int32)[:, None]
    return jnp.concatenate(
        [
            jnp.where(live, local, own),
            jnp.where(live, local, null_block),
            jnp.where(live, 0, 1).astype(jnp.int32),
        ],
        axis=1,
    )


def norm_in_place(rows_ref, gain_ref):
    strip = 16
    strips = BLOCK // strip

    def one(index, carry):
        block = index // strips
        rows = pl.ds(pl.multiple_of(lax.rem(index, strips) * strip, strip), strip)
        widened = rows_ref[block, rows, :].astype(jnp.float32)
        mean_square = jnp.mean(widened * widened, axis=-1, keepdims=True)
        normed = widened * lax.rsqrt(mean_square + 1e-06) * gain_ref[...]
        rows_ref[block, rows, :] = normed.astype(jnp.bfloat16)
        return carry

    lax.fori_loop(0, rows_ref.shape[0] * strips, one, 0)


def whole_kernel(
    groups_n, heads_n, slots_ref, q_gain, k_gain, q_in, k_in, v_in, o_out,
    q_rows, k_rows, q_ref, k_ref, v_ref, o_ref, ones_ref,
    load_sems, own_sems, send_sems, recv_sems, halo_send, halo_recv,
    relay_ref, relay_send, relay_recv,
):
    tm = lax.axis_index("tm")
    me = lax.axis_index("head")
    part = q_in.shape[0]
    width = q_ref.shape[2]
    per_frame = FRAME_BLOCKS // part
    frames_here = part * heads_n // FRAME_BLOCKS
    V, K, Q, O = range(4)

    def part_rows(index, base=0):
        return pl.ds(base + index * part, part)

    def part_lanes(index):
        return pl.ds(pl.multiple_of(index * width, width), width)

    def partner(offset):
        return lax.rem(me + offset, heads_n)

    def exchange(which, source, dest, base, offset):
        to = partner(offset)
        return pltpu.make_async_remote_copy(
            src_ref=source.at[:, :, part_lanes(to)],
            dst_ref=dest.at[part_rows(me, base)],
            send_sem=send_sems.at[which, offset],
            recv_sem=recv_sems.at[which, offset],
            device_id=(tm, to),
            device_id_type=pl.DeviceIdType.MESH,
        )

    def give_back(offset):
        to = partner(offset)
        return pltpu.make_async_remote_copy(
            src_ref=o_ref.at[part_rows(to)],
            dst_ref=o_out.at[:, :, part_lanes(me)],
            send_sem=send_sems.at[O, offset],
            recv_sem=recv_sems.at[O, offset],
            device_id=(tm, to),
            device_id_type=pl.DeviceIdType.MESH,
        )

    def own_copy(which, source, dest, base):
        return pltpu.make_async_copy(
            source.at[:, :, part_lanes(me)], dest.at[part_rows(me, base)], own_sems.at[which]
        )

    def halo(which, buffer, chunk):
        later = chunk // per_frame
        target = tm - 1 + 2 * later
        shift = (1 - 2 * later) * frames_here * FRAME_BLOCKS
        return pltpu.make_async_remote_copy(
            src_ref=buffer.at[part_rows(chunk, FRAME_BLOCKS)],
            dst_ref=buffer.at[part_rows(chunk, FRAME_BLOCKS + shift)],
            send_sem=halo_send.at[which, chunk],
            recv_sem=halo_recv.at[which, chunk],
            device_id=(target, me),
            device_id_type=pl.DeviceIdType.MESH,
        )

    def halo_goes(chunk):
        target = tm - 1 + 2 * (chunk // per_frame)
        return jnp.logical_and(target >= 0, target < groups_n)

    def halo_comes(chunk):
        origin = tm + 1 - 2 * (chunk // per_frame)
        return jnp.logical_and(origin >= 0, origin < groups_n)

    middle = groups_n // 2
    upper = tm // middle
    is_relay = lax.rem(tm, 2) == upper
    is_middle = jnp.logical_or(tm == middle - 1, tm == middle)

    def over_relay(chunk):
        return tm + chunk // per_frame == middle

    def first_leg(which, buffer, chunk):
        later = chunk // per_frame
        x = lax.rem(chunk, 4)
        place = which * 2 + lax.rem(chunk, per_frame) // 4
        return pltpu.make_async_remote_copy(
            src_ref=buffer.at[part_rows(chunk, FRAME_BLOCKS)],
            dst_ref=relay_ref.at[place],
            send_sem=halo_send.at[which, chunk],
            recv_sem=relay_recv.at[place],
            device_id=((1 - later) * (middle + 1) + 2 * x, me),
            device_id_type=pl.DeviceIdType.MESH,
        )

    def second_leg(which, buffer, index):
        later = 1 - upper
        place = which * 2 + index
        chunk = later * per_frame + index * 4 + lax.rem(tm, middle) // 2
        shift = (1 - 2 * later) * frames_here * FRAME_BLOCKS
        return pltpu.make_async_remote_copy(
            src_ref=relay_ref.at[place],
            dst_ref=buffer.at[part_rows(chunk, FRAME_BLOCKS + shift)],
            send_sem=relay_send.at[place],
            recv_sem=halo_recv.at[which, chunk],
            device_id=(middle - 1 + later, me),
            device_id_type=pl.DeviceIdType.MESH,
        )

    def relay(which, buffer):
        @pl.when(is_relay)
        def _():
            for index in range(2):
                first_leg(which, buffer, index * 4).wait_recv()
                second_leg(which, buffer, index).start()

    def send_halo(which, buffer, chunk):
        @pl.when(jnp.logical_and(halo_goes(chunk), jnp.logical_not(over_relay(chunk))))
        def _():
            halo(which, buffer, chunk).start()

        @pl.when(over_relay(chunk))
        def _():
            first_leg(which, buffer, chunk).start()

    k_load = pltpu.make_async_copy(k_in, k_rows, load_sems.at[0])
    q_load = pltpu.make_async_copy(q_in, q_rows, load_sems.at[1])
    k_load.start()
    q_load.start()

    barrier = pltpu.get_barrier_semaphore()
    for offset in range(1, heads_n):
        pl.semaphore_signal(
            barrier, inc=1, device_id=(tm, partner(offset)), device_id_type=pl.DeviceIdType.MESH
        )

    @pl.when(tm > 0)
    def _():
        pl.semaphore_signal(
            barrier, inc=1, device_id=(tm - 1, me), device_id_type=pl.DeviceIdType.MESH
        )

    @pl.when(tm < groups_n - 1)
    def _():
        pl.semaphore_signal(
            barrier, inc=1, device_id=(tm + 1, me), device_id_type=pl.DeviceIdType.MESH
        )

    @pl.when(is_relay)
    def _():
        for other in (middle - 1, middle):
            pl.semaphore_signal(
                barrier, inc=1, device_id=(other, me), device_id_type=pl.DeviceIdType.MESH
            )

    @pl.when(is_middle)
    def _():
        for x in range(4):
            for other in (2 * x, middle + 1 + 2 * x):
                pl.semaphore_signal(
                    barrier, inc=1, device_id=(other, me), device_id_type=pl.DeviceIdType.MESH
                )

    expected = heads_n - 1 + (tm > 0).astype(jnp.int32) + (tm < groups_n - 1).astype(jnp.int32)
    expected += 2 * is_relay.astype(jnp.int32) + 8 * is_middle.astype(jnp.int32)
    pl.semaphore_wait(barrier, expected)

    def each_chunk(body):
        def step(chunk, carry):
            body(chunk)
            return carry

        lax.fori_loop(0, heads_n, step, 0)

    line, lane_z = me // LINE, lax.rem(me, LINE)
    near, half = lax.rem((lane_z + 1) // 2, 2), lane_z // 2

    def each_target(body):
        def one(slot):
            crosses = 1 - lax.rem(slot // 8 + near, 2)
            ahead, other = lax.rem(slot, 8) // 2, lax.rem(slot, 2)
            z = lax.rem(half + crosses, 2) * 2 + lax.rem(lane_z + other, 2)
            to = lax.rem(line + ahead, heads_n // LINE) * LINE + z

            @pl.when(to != me)
            def _():
                body(lax.rem(to - me + heads_n, heads_n))

        each_chunk(one)

    def each_source(body):
        def one(slot):
            behind, same = lax.rem(slot, 8) // 2, lax.rem(slot, 2)
            side = lax.rem(half + 1 - same, 2)
            inner = lax.rem(same + slot // 8, 2)
            z = side * 3 + inner * (1 - 2 * side)
            source = lax.rem(line + heads_n // LINE - behind, heads_n // LINE) * LINE + z

            @pl.when(source != me)
            def _():
                body(lax.rem(me - source + heads_n, heads_n))

        each_chunk(one)

    v_args = (V, v_in, v_ref, FRAME_BLOCKS)
    k_args = (K, k_rows, k_ref, FRAME_BLOCKS)
    q_args = (Q, q_rows, q_ref, 0)
    each_target(lambda offset: exchange(*v_args, offset).start())
    v_own = own_copy(*v_args)
    v_own.start()
    k_load.wait()
    norm_in_place(k_rows, k_gain)
    each_target(lambda offset: exchange(*k_args, offset).start())
    k_own = own_copy(*k_args)
    k_own.start()
    q_load.wait()
    norm_in_place(q_rows, q_gain)
    q_own = own_copy(*q_args)
    q_own.start()
    v_ref[v_ref.shape[0] - 1] = jnp.zeros((BLOCK, width), jnp.bfloat16)
    ones_ref[0] = jnp.ones((BLOCK, HEAD_DIM), jnp.bfloat16)
    ones_ref[1] = jnp.zeros((BLOCK, HEAD_DIM), jnp.bfloat16)

    v_own.wait()
    send_halo(V, v_ref, me)

    def take_v(offset):
        exchange(*v_args, offset).wait_recv()
        send_halo(V, v_ref, lax.rem(me + heads_n - offset, heads_n))

    each_source(take_v)
    each_target(lambda offset: exchange(*q_args, offset).start())
    k_own.wait()
    send_halo(K, k_ref, me)

    def take_k(offset):
        exchange(*k_args, offset).wait_recv()
        send_halo(K, k_ref, lax.rem(me + heads_n - offset, heads_n))

    each_source(take_k)
    relay(V, v_ref)
    relay(K, k_ref)

    def take_halo(chunk):
        @pl.when(halo_comes(chunk))
        def _():
            halo(V, v_ref, chunk).wait_recv()
            halo(K, k_ref, chunk).wait_recv()

    each_chunk(take_halo)
    q_own.wait()
    def attend_part(source):
        def tile(index, carry):
            t = source * part + index
            attend_tile(q_ref, k_ref, v_ref, ones_ref, o_ref, slots_ref, t, KEEP // GROUP)
            return carry

        lax.fori_loop(0, part, tile, 0)

    attend_part(me)
    o_own = pltpu.make_async_copy(
        o_ref.at[part_rows(me)], o_out.at[:, :, part_lanes(me)], own_sems.at[O]
    )
    o_own.start()

    def serve(offset):
        exchange(*q_args, offset).wait_recv()
        attend_part(lax.rem(me + heads_n - offset, heads_n))
        give_back(heads_n - offset).start()

    each_source(serve)

    def finish(offset):
        for args in (v_args, k_args, q_args):
            exchange(*args, offset).wait_send()
        give_back(offset).wait_send()

    each_target(finish)

    def finish_halo(chunk):
        @pl.when(halo_goes(chunk))
        def _():
            halo(V, v_ref, chunk).wait_send()
            halo(K, k_ref, chunk).wait_send()

    each_chunk(finish_halo)
    @pl.when(is_relay)
    def _():
        for which, buffer in ((V, v_ref), (K, k_ref)):
            for index in range(2):
                second_leg(which, buffer, index).wait_send()

    o_own.wait()
    each_target(lambda offset: give_back(offset).wait_recv())


def shards(queries, key_in, values_in, query_gain, key_gain, keep_list, counts):
    groups_n, heads_n = lax.axis_size("tm"), lax.axis_size("head")
    rows, features = queries.shape
    part = rows // BLOCK
    width = features // heads_n
    local_blocks = part * heads_n
    reach = local_blocks + 2 * FRAME_BLOCKS
    first_block = lax.axis_index("tm") * local_blocks - FRAME_BLOCKS
    slots = slot_table(keep_list, counts, first_block, reach)
    scalar = pl.BlockSpec(memory_space=pltpu.SMEM)
    vector = pl.BlockSpec(memory_space=pltpu.VMEM)
    whole = pl.BlockSpec(memory_space=pl.ANY)
    dma = pltpu.SemaphoreType.DMA
    blocks = (part, BLOCK, features)
    bf16 = jnp.bfloat16
    attended = pl.pallas_call(
        functools.partial(whole_kernel, groups_n, heads_n),
        out_shape=jax.ShapeDtypeStruct(blocks, bf16),
        in_specs=[scalar] + [vector] * 2 + [whole] * 3,
        out_specs=whole,
        scratch_shapes=[
            pltpu.VMEM(blocks, bf16),
            pltpu.VMEM(blocks, bf16),
            pltpu.VMEM((local_blocks, BLOCK, width), bf16),
            pltpu.VMEM((reach, BLOCK, width), bf16),
            pltpu.VMEM((reach + 1, BLOCK, width), bf16),
            pltpu.VMEM((local_blocks, BLOCK, width), bf16),
            pltpu.VMEM((2, BLOCK, HEAD_DIM), bf16),
            dma((2,)),
            dma((4,)),
            dma((4, heads_n)),
            dma((4, heads_n)),
            dma((2, heads_n)),
            dma((2, heads_n)),
            pltpu.VMEM((4, part, BLOCK, width), bf16),
            dma((4,)),
            dma((4,)),
        ],
        compiler_params=pltpu.CompilerParams(
            collective_id=0, has_side_effects=True, vmem_limit_bytes=48 * 2**20
        ),
        cost_estimate=pl.CostEstimate(
            flops=local_blocks * BLOCK * KEEP * BLOCK * width * 4,
            bytes_accessed=8 * rows * features,
            transcendentals=local_blocks * BLOCK * KEEP * BLOCK * 2,
        ),
    )(
        slots, query_gain.reshape(1, -1), key_gain.reshape(1, -1),
        queries.reshape(blocks), key_in.reshape(blocks), values_in.reshape(blocks),
    )
    return attended.reshape(rows, features)


def solution(mesh):
    placed = (
        P(("tm", "head"), None),
        P(("tm", "head"), None),
        P(("tm", "head"), None),
        P(),
        P(),
        P("tm", None),
        P("tm"),
    )
    return jax.shard_map(
        shards, mesh=mesh, in_specs=placed, out_specs=P(("tm", "head"), None), check_vma=False
    )
```

time: 863 us -> 222 us (0.26)
  local copies, waits for them, and re-layouts: 292 us -> 5.14 us
  Pallas kernels: 0 us -> 214 us
  other arithmetic: 172 us -> 0.82 us
  matrix products: 166 us -> 0 us
  waiting for transfers between devices: 144 us -> 0 us
  blocking collectives: 56.2 us -> 0 us
  starting transfers between devices: 26.8 us -> 0 us
    pallas_call x0 -> x1, Pallas kernels: none -> 214 us  [shards(): pl.pallas_call(functools.partial(whole_kernel, groups_n, heads_n), out_sh...]
    gather x32 -> x0, local copies, waits for them, and re-layouts: 206 us -> none  [one_slot(): gathered = jnp.take(key_value_blocks, block_ids, axis=1)]
    dot_general x64 -> x0, matrix products: 166 us -> none  [the longest x32 123 us: one_slot(): jnp.einsum('thqk,tkhd->tqhd', weights, gathered[1], preferred_element_typ...]
    all_to_all x3 -> x0, waiting for transfers between devices: 144 us -> none  [the longest x1 51.2 us: shards(): lax.all_to_all(query_normed, 'head', split_axis=1, concat_axis=0, tiled=T...]
    select_n x32 -> x1, other arithmetic: 83.9 us -> 0.74 us  [slot_table(): jnp.where(live, local, own)]
    all_to_all x1 -> x0, blocking collectives: 56.2 us -> none  [shards(): lax.all_to_all(mixed_out, 'head', split_axis=0, concat_axis=1, tiled=True)]
    reduce_sum x34 -> x0, other arithmetic: 53.5 us -> none  [the longest x32 52.4 us: one_slot(): run_sum = run_sum * rescale + jnp.sum(weights.astype(jnp.float32), axis=-1)]
    while x160 -> x0, local copies, waits for them, and re-layouts: 30.4 us -> none
  transfers between devices with their start and end apart: 5 -> 0, of which waited for: 3 -> 0; matrix products, arithmetic and copies ran while one was open for 3% -> 0% of each run, Pallas kernels for 0% -> 0%
where the time goes in v2:
time: 222 us; the launch traced here: 220 us
  Pallas kernels  214 us (96%)
  local copies, waits for them, and re-layouts  5.14 us (2%)
    pallas_call x1, Pallas kernels, shards(): pl.pallas_call(functools.partial(whole_kernel, groups_n, heads_n), out_sh...  214 us
    unnamed x8, local copies, waits for them, and re-layouts  5.14 us

profile of v2, /device:TPU:7, one launch (start us, length us, event | category | flops | bytes accessed | tf_op | source)
XLA Modules:
  0.0 219.6 jit_solution(5334041385941492053)
XLA Ops:
  0.0 0.8 copy.8
  0.8 0.7 fusion.2
  1.5 0.1 pad_add_fusion.slots_ref
  1.6 0.0 copy-start
  1.6 1.6 copy-done
  3.2 0.0 copy-start.1
  3.2 0.7 copy-done.1
  3.9 0.0 copy-start.2
  3.9 0.7 copy-done.2
  4.7 213.6 %shard_map.73 = bf16[4,64,4096]{2,1,0:T(8,128)(2,1)S(1)} custom-call(s32[64,96]{1,0:T(8,128)S(1)} %pad_add_fusion.slots_ref, f32[1,4096]{1,0:T(1,128)S(1)} %bitcast.8, f32[1,4096]{1,0:T(1,128)S(1)} %bitcast.9, bf16[4,64,4096]{2,1,0:T(8,128)(2,1)S(1)} %bitcast.7, bf16[4,64,4096]{2,1,0:T(8,128)(2,1)} %bitcast.10, bf16[4,64,4096]{2,1,0:T(8,128)(2,1)} %bitcast.11), custom_call_target="tpu_custom_call" | custom-call | flops 8589934592 | bytes 8388608 | tf_op jit(solution)/shard_map/pallas_call | solution.py:396
  218.2 1.3 copy.10
  (1 shorter events, 0.0 us)
Async XLA Ops:
  1.6 1.6 copy-start
  3.2 0.7 copy-start.1
  3.9 0.7 copy-start.2

commit v3 on v2

--- a/solution.py
+++ b/solution.py
@@ -13,6 +13,7 @@
 BLOCK = 64
 FRAME_BLOCKS = 32
 KEEP = 32
+PAIR = 2
 LINE = 4
 GROUP = 4
 EXP2_SCALE = HEAD_DIM ** (-0.5) * math.log2(math.e)
@@ -264,7 +265,7 @@
             crosses = 1 - lax.rem(slot // 8 + near, 2)
             ahead, other = lax.rem(slot, 8) // 2, lax.rem(slot, 2)
             z = lax.rem(half + crosses, 2) * 2 + lax.rem(lane_z + other, 2)
-            to = lax.rem(line + ahead, heads_n // LINE) * LINE + z
+            to = lax.rem(me + slot, heads_n)
 
             @pl.when(to != me)
             def _():
@@ -278,7 +279,7 @@
             side = lax.rem(half + 1 - same, 2)
             inner = lax.rem(same + slot // 8, 2)
             z = side * 3 + inner * (1 - 2 * side)
-            source = lax.rem(line + heads_n // LINE - behind, heads_n // LINE) * LINE + z
+            source = lax.rem(me + heads_n - slot, heads_n)
 
             @pl.when(source != me)
             def _():
@@ -313,7 +314,6 @@
         send_halo(V, v_ref, lax.rem(me + heads_n - offset, heads_n))
 
     each_source(take_v)
-    each_target(lambda offset: exchange(*q_args, offset).start())
     k_own.wait()
     send_halo(K, k_ref, me)
 
@@ -321,9 +321,10 @@
         exchange(*k_args, offset).wait_recv()
         send_halo(K, k_ref, lax.rem(me + heads_n - offset, heads_n))
 
+    relay(V, v_ref)
     each_source(take_k)
-    relay(V, v_ref)
     relay(K, k_ref)
+    each_target(lambda offset: exchange(*q_args, offset).start())
 
     def take_halo(chunk):
         @pl.when(halo_comes(chunk))
@@ -335,11 +336,12 @@
     q_own.wait()
     def attend_part(source):
         def tile(index, carry):
-            t = source * part + index
-            attend_tile(q_ref, k_ref, v_ref, ones_ref, o_ref, slots_ref, t, KEEP // GROUP)
+            for more in range(PAIR):
+                t = source * part + index * PAIR + more
+                attend_tile(q_ref, k_ref, v_ref, ones_ref, o_ref, slots_ref, t, KEEP // GROUP)
             return carry
 
-        lax.fori_loop(0, part, tile, 0)
+        lax.fori_loop(0, part // PAIR, tile, 0)
 
     attend_part(me)
     o_own = pltpu.make_async_copy(

time: 222 us -> 214 us (0.964)
  Pallas kernels: 214 us -> 207 us
    pallas_call x1, Pallas kernels: 214 us -> 207 us  [shards(): pl.pallas_call(functools.partial(whole_kernel, groups_n, heads_n), out_sh...]
where the time goes in v3:
time: 214 us; the launch traced here: 213 us
  Pallas kernels  207 us (97%)
  local copies, waits for them, and re-layouts  5.14 us (2%)
    pallas_call x1, Pallas kernels, shards(): pl.pallas_call(functools.partial(whole_kernel, groups_n, heads_n), out_sh...  207 us
    unnamed x8, local copies, waits for them, and re-layouts  5.14 us

profile of v3, /device:TPU:7, one launch (start us, length us, event | category | flops | bytes accessed | tf_op | source)
XLA Modules:
  0.0 213.1 jit_solution(2178834963746519299)
XLA Ops:
  0.0 0.8 copy.8
  0.8 0.7 fusion.2
  1.5 0.1 pad_add_fusion.slots_ref
  1.6 0.0 copy-start
  1.6 1.6 copy-done
  3.2 0.0 copy-start.1
  3.2 0.7 copy-done.1
  3.9 0.0 copy-start.2
  3.9 0.7 copy-done.2
  4.7 207.1 %shard_map.73 = bf16[4,64,4096]{2,1,0:T(8,128)(2,1)S(1)} custom-call(s32[64,96]{1,0:T(8,128)S(1)} %pad_add_fusion.slots_ref, f32[1,4096]{1,0:T(1,128)S(1)} %bitcast.8, f32[1,4096]{1,0:T(1,128)S(1)} %bitcast.9, bf16[4,64,4096]{2,1,0:T(8,128)(2,1)S(1)} %bitcast.7, bf16[4,64,4096]{2,1,0:T(8,128)(2,1)} %bitcast.10, bf16[4,64,4096]{2,1,0:T(8,128)(2,1)} %bitcast.11), custom_call_target="tpu_custom_call" | custom-call | flops 8589934592 | bytes 8388608 | tf_op jit(solution)/shard_map/pallas_call | solution.py:398
  211.8 1.3 copy.10
  (1 shorter events, 0.0 us)
Async XLA Ops:
  1.6 1.6 copy-start
  3.2 0.7 copy-start.1
  3.9 0.7 copy-start.2

commit v4 on v3

--- a/solution.py
+++ b/solution.py
@@ -13,7 +13,7 @@
 BLOCK = 64
 FRAME_BLOCKS = 32
 KEEP = 32
-PAIR = 2
+PAIR = 4
 LINE = 4
 GROUP = 4
 EXP2_SCALE = HEAD_DIM ** (-0.5) * math.log2(math.e)

time: 214 us -> 214 us (level)
  no operation moved by 1% of the time
where the time goes in v4:
time: 214 us; the launch traced here: 213 us
  Pallas kernels  207 us (97%)
  local copies, waits for them, and re-layouts  5.14 us (2%)
    pallas_call x1, Pallas kernels, shards(): pl.pallas_call(functools.partial(whole_kernel, groups_n, heads_n), out_sh...  207 us
    unnamed x8, local copies, waits for them, and re-layouts  5.14 us

profile of v4, /device:TPU:7, one launch (start us, length us, event | category | flops | bytes accessed | tf_op | source)
XLA Modules:
  0.0 212.7 jit_solution(3613909475722186673)
XLA Ops:
  0.0 0.8 copy.8
  0.8 0.7 fusion.2
  1.5 0.1 pad_add_fusion.slots_ref
  1.6 0.0 copy-start
  1.6 1.6 copy-done
  3.2 0.0 copy-start.1
  3.2 0.7 copy-done.1
  3.9 0.0 copy-start.2
  3.9 0.7 copy-done.2
  4.7 206.7 %shard_map.73 = bf16[4,64,4096]{2,1,0:T(8,128)(2,1)S(1)} custom-call(s32[64,96]{1,0:T(8,128)S(1)} %pad_add_fusion.slots_ref, f32[1,4096]{1,0:T(1,128)S(1)} %bitcast.8, f32[1,4096]{1,0:T(1,128)S(1)} %bitcast.9, bf16[4,64,4096]{2,1,0:T(8,128)(2,1)S(1)} %bitcast.7, bf16[4,64,4096]{2,1,0:T(8,128)(2,1)} %bitcast.10, bf16[4,64,4096]{2,1,0:T(8,128)(2,1)} %bitcast.11), custom_call_target="tpu_custom_call" | custom-call | flops 8589934592 | bytes 8388608 | tf_op jit(solution)/shard_map/pallas_call | solution.py:398
  211.4 1.3 copy.10
  (1 shorter events, 0.0 us)
Async XLA Ops:
  1.6 1.6 copy-start
  3.2 0.7 copy-start.1
  3.9 0.7 copy-start.2
